TPU v7x, 32 devices: a whole 2x2x4 slice. The times are simulated.
32 devices in a mesh: groups: 2 (over y), tensor: 4 (over z), bank: 2 (over x), pipe: 2 (over core).
Axes of the slice: x: 2, y: 2, z: 4, core: 2. Of those that a mesh axis runs over, the one named last changes fastest.
Arguments:
- x_in: bfloat16 [4096, 5120], P(('groups', 'bank', 'pipe'), 'tensor'), parts along dimension 0, may hold values from -6 to 6
- grad_out: bfloat16 [4096, 5120], P(('groups', 'bank', 'pipe'), 'tensor'), parts along dimension 0, may hold values from -6 to 6
- gate_pre: bfloat16 [4096, 17408], P(('groups', 'bank', 'pipe'), 'tensor'), parts along dimension 0, may hold values from -6 to 6
- up_pre: bfloat16 [4096, 17408], P(('groups', 'bank', 'pipe'), 'tensor'), parts along dimension 0, may hold values from -6 to 6
- w_down: bfloat16 [17408, 5120], P('tensor', 'pipe'), may hold values from -0.046875 to 0.046875
- proj_in: bfloat16 [5120, 64], P('tensor'), may hold values from -0.078125 to 0.078125
- proj_ff: bfloat16 [17408, 64], P('tensor'), may hold values from -0.046875 to 0.046875
- resp_mask: int32 [4096], P(('groups', 'bank', 'pipe')), parts along dimension 0, may hold values 0 or 1
- doc_lengths: int32 [16], P('groups'), parts along dimension 0, may hold values from 1 to 1024, 2048 in all
- owner: int32 [16], P('groups'), parts along dimension 0, may hold values from 0 to 1, as said below
- bank_grads: bfloat16 [2, 256, 12288], P('bank', 'pipe', 'tensor'), may hold values from -0.0034179688 to 0.0034179688
Outputs:
- scores: float32 [16, 256], P('groups', 'pipe'), parts along dimension 0
There are 2 independent parts, one for each index of `groups`. A program takes and returns all parts, laid end to end along the dimension named above; an argument that names none is the same for every part. Nothing has to cross between parts.
Inputs may be any that keep to these rules, and one draw needn't show every extreme that they name: Each owner is named by exactly 4 examples. `doc_lengths`: the lengths sum to 2048.
All inputs are finite; a program needn't handle non-finite values. No bound on the sum of `resp_mask` on one device may be relied on, other than what follows from the above.
Results may differ from a plain program's by a relative error of at most 0.0029.
Values may be sent and summed in bfloat16 or wider, within the bound.
A program may use at most 128 MiB of HBM per device.

v0:
```python
import jax
import jax.numpy as jnp
import numpy as np
from jax import lax
from jax.sharding import PartitionSpec as P


def body(
    x_in,
    grad_out,
    gate_pre,
    up_pre,
    w_down,
    proj_in,
    proj_ff,
    resp_mask,
    doc_lengths,
    owner,
    bank_grads,
):
    rows_here = x_in.shape[0]
    proj_rank = proj_in.shape[1]
    contract_last = (((1,), (1,)), ((), ()))
    full_rows = lax.all_gather(grad_out, "tensor", axis=1, tiled=True)
    paired = lax.all_to_all(full_rows, "pipe", split_axis=1, concat_axis=0, tiled=True)
    hidden_grad = lax.psum_scatter(
        lax.dot_general(paired, w_down, contract_last, preferred_element_type=jnp.float32),
        "pipe",
        scatter_dimension=0,
        tiled=True,
    )
    gate_val = gate_pre.astype(jnp.float32)
    up_val = up_pre.astype(jnp.float32)
    sigmoid_gate = jax.nn.sigmoid(gate_val)
    activated = gate_val * sigmoid_gate
    slope = sigmoid_gate * (1.0 + gate_val * (1.0 - sigmoid_gate))
    hidden = (activated * up_val).astype(jnp.bfloat16)
    up_grad = (hidden_grad * activated).astype(jnp.bfloat16)
    gate_grad = (hidden_grad * up_val * slope).astype(jnp.bfloat16)
    wide_side = jnp.stack([hidden, up_grad, gate_grad])
    wide_proj = jnp.einsum("stf,fr->srt", wide_side, proj_ff, preferred_element_type=jnp.float32)
    narrow_side = jnp.stack([x_in, grad_out])
    narrow_proj = jnp.einsum(
        "std,dr->srt", narrow_side, proj_in, preferred_element_type=jnp.float32
    )
    partials = jnp.concatenate([wide_proj, narrow_proj], axis=0)
    projected = lax.psum(partials, "tensor")
    stacked = projected.reshape(5 * proj_rank, rows_here)
    kron_part = bank_grads.shape[2]
    square = proj_rank * proj_rank
    module_ids = np.repeat(np.arange(3), square)
    inner_ids = np.arange(3 * square) % square
    left_table = np.array([0, 3, 3])[module_ids] * proj_rank + inner_ids // proj_rank
    right_table = np.array([4, 1, 2])[module_ids] * proj_rank + inner_ids % proj_rank
    first_entry = lax.axis_index("tensor") * kron_part
    left_ids = lax.dynamic_slice_in_dim(jnp.asarray(left_table, jnp.int32), first_entry, kron_part)
    right_ids = lax.dynamic_slice_in_dim(
        jnp.asarray(right_table, jnp.int32), first_entry, kron_part
    )
    products = jnp.take(stacked, left_ids, axis=0) * jnp.take(stacked, right_ids, axis=0)
    offset = lax.axis_index(("bank", "pipe")) * rows_here
    positions = offset + jnp.arange(rows_here, dtype=jnp.int32)
    doc_ends = jnp.cumsum(doc_lengths)
    starts = doc_ends - doc_lengths
    inside = (positions[:, None] >= starts[None, :]) & (positions[:, None] < doc_ends[None, :])
    member = inside.astype(jnp.float32) * resp_mask.astype(jnp.float32)[:, None]
    grad_part = lax.dot_general(
        member,
        products,
        (((0,), (1,)), ((), ())),
        precision=lax.Precision.HIGHEST,
        preferred_element_type=jnp.float32,
    )
    example_grads = lax.psum(grad_part, ("bank", "pipe"))
    own_rows = bank_grads[0].astype(jnp.float32)
    partial_value = lax.dot_general(
        example_grads,
        own_rows,
        contract_last,
        precision=lax.Precision.HIGHEST,
        preferred_element_type=jnp.float32,
    )
    owned = (owner == lax.axis_index("bank")).astype(jnp.float32)[:, None]
    scores = lax.psum(partial_value * owned, ("tensor", "bank"))
    return scores


def solution(mesh):
    return jax.shard_map(
        body,
        mesh=mesh,
        in_specs=(
            P(("groups", "bank", "pipe"), "tensor"),
            P(("groups", "bank", "pipe"), "tensor"),
            P(("groups", "bank", "pipe"), "tensor"),
            P(("groups", "bank", "pipe"), "tensor"),
            P("tensor", "pipe"),
            P("tensor", None),
            P("tensor", None),
            P(("groups", "bank", "pipe")),
            P("groups"),
            P("groups"),
            P("bank", "pipe", "tensor"),
        ),
        out_specs=P("groups", "pipe"),
        check_vma=False,
    )
```

profile of v0, /device:TPU:0, one launch (start us, length us, event | category | flops | bytes accessed | tf_op | source)
XLA Modules:
  0.0 342.8 jit_solution(4638233036490334645)
XLA Ops:
  6.5 2.5 copy.14
  9.1 0.0 all-gather.2.cloned.1.call-update
  9.1 0.0 reduce-scatter.2.cloned.1.call-start
  9.1 100.9 %all-gather.2.cloned.1.call-done = bf16[512,5120]{0,1:T(8,128)(2,1)} async-done(((bf16[512,1280]{0,1:T(8,128)(2,1)}), bf16[512,5120]{0,1:T(8,128)(2,1)}) %all-gather.2.cloned.1.call-update) | async-done | bytes 5242896 | tf_op jit(solution)/shard_map/all_gather | solution.py:24
  110.0 13.6 %all_to_all.19 = bf16[512,2,2560]{0,2,1:T(8,128)(2,1)} all-to-all(bf16[512,2,2560]{0,2,1:T(8,128)(2,1)} %bitcast.32), channel_id=1, replica_groups=mesh['groups'=2,'tensor'=4,'bank'=2,'pipe'=2] {'pipe'}, dimensions={1} | all-to-all | bytes 10485760 | tf_op jit(solution)/shard_map/all_to_all | solution.py:25
  123.6 7.8 %copy.15 = bf16[2,512,2560]{2,1,0:T(8,128)(2,1)} copy(bf16[2,512,2560]{1,2,0:T(8,128)(2,1)} %bitcast.31) | data formatting | bytes 10485760 | tf_op jit(solution)/shard_map/all_to_all | solution.py:25
  131.4 30.7 %fusion.56 = f32[1024,4352]{1,0:T(8,128)} fusion(bf16[1024,2560]{1,0:T(8,128)(2,1)} %bitcast.33, bf16[4352,2560]{1,0:T(8,128)(2,1)} %param.19), kind=kOutput, calls=%fused_computation.68 | convolution fusion | flops 22817013760 | bytes 45350912 | tf_op jit(solution)/shard_map/dot_general | solution.py:27
  162.1 0.0 all-reduce.3.cloned.1.call-start
  162.1 1.2 copy-done.2
  163.4 2.2 fusion.29
  165.6 22.1 %reduce-scatter.2.cloned.1.call-done = f32[512,4352]{1,0:T(8,128)} async-done(((f32[1024,4352]{1,0:T(8,128)}), f32[512,4352]{1,0:T(8,128)}) %reduce-scatter.2.cloned.1.call-update) | async-done | bytes 8912912 | tf_op jit(solution)/shard_map/reduce_scatter | solution.py:26
  187.7 8.6 %fusion.16 = (bf16[1,512,4352]{2,1,0:T(8,128)(2,1)S(1)}, bf16[1,512,4352]{2,1,0:T(8,128)(2,1)S(1)}, bf16[1,512,4352]{2,1,0:T(8,128)(2,1)S(1)}) fusion(f32[512,4352]{1,0:T(8,128)} %reduce-scatter.2.cloned.1.call-done, bf16[512,4352]{1,0:T(8,128)(2,1)} %param.17, bf16[512,4352]{1,0:T(8,128)(2,1)} %param.18), kind=kLoop, calls=%fused_computation.25 | loop fusion | flops 37879808 | bytes 31195136 | tf_op jit(solution)/shard_map/stack | solution.py:40
  196.4 4.4 %fusion.26 = f32[3,64,512]{2,1,0:T(8,128)S(1)} fusion(bf16[1,512,4352]{2,1,0:T(8,128)(2,1)S(1)} %get-tuple-element.7, bf16[1,512,4352]{2,1,0:T(8,128)(2,1)S(1)} %get-tuple-element.6, bf16[1,512,4352]{2,1,0:T(8,128)(2,1)S(1)} %get-tuple-element.8, bf16[4352,64]{0,1:T(8,128)(2,1)S(1)} %copy-done.6), kind=kOutput, calls=%fused_computation.35 | convolution fusion | flops 869007360 | bytes 14319616 | tf_op jit(solution)/shard_map/stf,fr->srt/dot_general | solution.py:41
  200.8 0.9 pad_maximum_fusion
  201.7 0.0 all-reduce.3.cloned.1.call-update
  201.7 0.2 all-reduce.5.cloned.1.call-start
  201.9 0.2 reduce-window.8
  202.2 41.5 %all-reduce.3.cloned.1.call-done = f32[320,512]{1,0:T(8,128)} async-done(((f32[320,512]{1,0:T(8,128)}), f32[320,512]{1,0:T(8,128)}) %all-reduce.3.cloned.1.call-update) | async-done | bytes 655376 | tf_op jit(solution)/shard_map/psum | solution.py:47
  243.8 14.9 %gather_fusion = f32[3072,512]{1,0:T(8,128)} fusion(f32[320,512]{1,0:T(8,128)} %all-reduce.3.cloned.1.call-done, s32[3072]{0:T(1024)S(1)} %get-tuple-element.10), kind=kCustom, calls=%fused_computation.clone | custom fusion | bytes 12595200 | tf_op jit(solution)/shard_map/jit(_take)/gather | solution.py:60
  258.7 12.9 %gather_fusion.1 = f32[3072,512]{1,0:T(8,128)} fusion(f32[320,512]{1,0:T(8,128)S(1)} %copy-done.1, s32[3072]{0:T(1024)S(1)} %get-tuple-element.9), kind=kCustom, calls=%fused_computation.1.clone | custom fusion | bytes 12595200 | tf_op jit(solution)/shard_map/jit(_take)/gather | solution.py:60
  271.6 11.2 %fusion.14 = f32[8,3072]{1,0:T(8,128)} fusion(f32[3072,512]{1,0:T(8,128)} %gather_fusion.1, f32[3072,512]{1,0:T(8,128)} %gather_fusion, pred[3072]{0:T(1024)(128)(4,1)S(1)} %get-tuple-element.12, pred[3072]{0:T(1024)(128)(4,1)S(1)} %get-tuple-element.11, f32[512]{0:T(512)S(1)} %convert_element_type.23, s32[8]{0:T(128)S(1)} %bitcast.36, ...), kind=kOutput, calls=%fused_computation.23 | convolution fusion | flops 155729920 | bytes 12691520 | tf_op jit(solution)/shard_map/dot_general | solution.py:67
  282.8 30.9 %all-reduce.5.cloned.1.call-done = f32[8,3072]{1,0:T(8,128)} async-done(((f32[8,3072]{1,0:T(8,128)}), f32[8,3072]{1,0:T(8,128)}) %all-reduce.5.cloned.1.call-update) | async-done | bytes 98320 | tf_op jit(solution)/shard_map/psum | solution.py:74
  313.7 1.6 convolution_multiply_fusion
  315.3 21.0 %psum.23 = f32[8,128]{1,0:T(8,128)} all-reduce(f32[8,128]{1,0:T(8,128)S(1)} %convolution_multiply_fusion), channel_id=1, replica_groups=mesh['groups'=2,'tensor'=4,'bank'=2,'pipe'=2] {'tensor','bank'}, use_global_device_ids=true, to_apply=%region_4.6 | all-reduce | flops 1024 | bytes 8192 | tf_op jit(solution)/shard_map/psum | solution.py:84
  (28 shorter events, 0.1 us)
Async XLA Ops:
  6.5 307.2 %copy-start = (bf16[1,128,3072]{2,1,0:T(8,128)(2,1)S(1)}, bf16[1,128,3072]{2,1,0:T(8,128)(2,1)}, u32[]{:S(2)}) copy-start(bf16[1,128,3072]{2,1,0:T(8,128)(2,1)} %param.25) | copy-start | bytes 2359300
  6.5 103.5 %all-gather.2.cloned.1.call-start = ((), (), s32[]{:S(2)}) async-start(), calls=%async_computation.2 | async-start | bytes 6553600 | tf_op jit(solution)/shard_map/all_gather | solution.py:24
  9.1 178.6 %reduce-scatter.2.cloned.1.call-start = ((), (), s32[]{:S(2)}) async-start(), calls=%async_computation.3 | async-start | bytes 26738688 | tf_op jit(solution)/shard_map/reduce_scatter | solution.py:26
  162.0 1.3 copy-start.2
  162.0 1.3 copy-start.7
  162.1 81.7 %all-reduce.3.cloned.1.call-start = ((), (), s32[]{:S(2)}) async-start(), calls=%async_computation.4 | async-start | bytes 1310720 | tf_op jit(solution)/shard_map/psum | solution.py:47
  165.6 30.8 %copy-start.6 = (bf16[4352,64]{0,1:T(8,128)(2,1)S(1)}, bf16[4352,64]{0,1:T(8,128)(2,1)}, u32[]{:S(2)}) copy-start(bf16[4352,64]{0,1:T(8,128)(2,1)} %param.21) | copy-start | bytes 1671172
  196.4 5.6 %copy-start.8 = (s32[8]{0:T(128)S(1)}, s32[8]{0:T(128)}, u32[]{:S(2)}) copy-start(s32[8]{0:T(128)} %param.23) | copy-start | bytes 100
  196.4 5.8 %copy-start.5 = (s32[512]{0:T(512)S(1)}, s32[512]{0:T(512)}, u32[]{:S(2)}) copy-start(s32[512]{0:T(512)} %param.22) | copy-start | bytes 6148
  196.4 5.8 %copy-start.3 = (s32[12288]{0:T(1024)S(1)}, s32[12288]{0:T(1024)}, u32[]{:S(2)}) copy-start(s32[12288]{0:T(1024)} %constant.42.clone) | copy-start | bytes 147460
  196.4 5.8 %copy-start.4 = (s32[12288]{0:T(1024)S(1)}, s32[12288]{0:T(1024)}, u32[]{:S(2)}) copy-start(s32[12288]{0:T(1024)} %constant.43.clone) | copy-start | bytes 147460
  201.7 112.0 %all-reduce.5.cloned.1.call-start = ((), (), s32[]{:S(2)}) async-start(), calls=%async_computation.5 | async-start | bytes 196608 | tf_op jit(solution)/shard_map/psum | solution.py:74
  243.8 14.9 %copy-start.1 = (f32[320,512]{1,0:T(8,128)S(1)}, f32[320,512]{1,0:T(8,128)}, u32[]{:S(2)}) copy-start(f32[320,512]{1,0:T(8,128)} %all-reduce.3.cloned.1.call-done) | copy-start | bytes 1966084
  271.6 11.2 %copy-start.9 = (s32[8]{0:T(128)S(1)}, s32[8]{0:T(128)}, u32[]{:S(2)}) copy-start(s32[8]{0:T(128)} %param.24) | copy-start | bytes 100
Sparse Core Ops, SparseCore 0:
  9.2 100.7 all-gather.1
  162.2 25.4 reduce-scatter.1
  201.8 41.9 all-reduce.2
  282.9 30.7 all-reduce.4
where the time goes:
time: 343 us
  waiting for transfers between devices  196 us (57%)
  matrix products  50 us (15%)
  local copies, waits for them, and re-layouts  39.4 us (11%)
  blocking collectives  34.6 us (10%)
  between operations  13.3 us (4%)
  other arithmetic  9.77 us (3%)
    all_gather x1, waiting for transfers between devices, body(): full_rows = lax.all_gather(grad_out, 'tensor', axis=1, tiled=True)  101 us
    psum x1, waiting for transfers between devices, body(): projected = lax.psum(partials, 'tensor')  41.5 us
    psum x1, waiting for transfers between devices, body(): example_grads = lax.psum(grad_part, ('bank', 'pipe'))  30.9 us
    dot_general x1, matrix products, body(): lax.dot_general(paired, w_down, contract_last, preferred_element_type=jnp...  30.7 us
    reduce_scatter x1, waiting for transfers between devices, body(): lax.psum_scatter(lax.dot_general(paired, w_down, contract_last, preferred...  22.1 us
    psum x1, blocking collectives, body(): scores = lax.psum(partial_value * owned, ('tensor', 'bank'))  21 us
    gather x1, local copies, waits for them, and re-layouts, body(): jnp.take(stacked, left_ids, axis=0) * jnp.take(stacked, right_ids, axis=0)  14.9 us
    all_to_all x1, blocking collectives, body(): lax.all_to_all(full_rows, 'pipe', split_axis=1, concat_axis=0, tiled=True)  13.6 us
  transfers between devices with their start and end apart: 4, of which 4 were waited for; matrix products, arithmetic and copies ran while one was open for 1% of the time, Pallas kernels for 0%

commit v1 on v0

--- a/solution.py
+++ b/solution.py
@@ -1,8 +1,18 @@
+import functools
 import jax
 import jax.numpy as jnp
 import numpy as np
 from jax import lax
 from jax.sharding import PartitionSpec as P
+from jax.experimental import pallas as pl
+from jax.experimental.pallas import tpu as pltpu
+
+MESH = pl.DeviceIdType.MESH
+VMEM = pl.BlockSpec(memory_space=pltpu.VMEM)
+CAP = 320
+PIECES = 4
+LIMIT = 56 * 1024 * 1024
+LAST = (((1,), (1,)), ((), ()))
 
 
 def body(
@@ -85,9 +95,491 @@
     return scores
 
 
+def params(cid, **more):
+    return pltpu.CompilerParams(
+        collective_id=cid, has_side_effects=True, vmem_limit_bytes=LIMIT, **more
+    )
+
+
+def greet(devices):
+    barrier = pltpu.get_barrier_semaphore()
+    for device in devices:
+        pl.semaphore_signal(barrier, inc=1, device_id=device, device_id_type=MESH)
+    pl.semaphore_wait(barrier, len(devices))
+
+
+def gather_kernel(nz, half, pick, grad, x_in, proj, buf, narrow, packed, own_sem, fwd_sem, recv_sem):
+    z, c = lax.axis_index("tensor"), lax.axis_index("pipe")
+    other = 1 - c
+    dest, place = z // half, z % half
+    rows = packed.shape[0] // PIECES
+    barrier = pltpu.get_barrier_semaphore()
+    pl.semaphore_signal(barrier, inc=1, device_id={"pipe": other}, device_id_type=MESH)
+    for step in (-1, 1):
+
+        @pl.when((z + step >= 0) & (z + step < nz))
+        def _():
+            for core in range(2):
+                pl.semaphore_signal(
+                    barrier,
+                    inc=1,
+                    device_id={"tensor": z + step, "pipe": core},
+                    device_id_type=MESH,
+                )
+
+    inner = jnp.where((z > 0) & (z < nz - 1), 5, 3)
+    packed[...] = jnp.dot(pick[...], grad[...], preferred_element_type=jnp.float32).astype(
+        jnp.bfloat16
+    )
+    pl.semaphore_wait(barrier, inner)
+
+    def piece(q):
+        return pl.ds(q * rows, rows)
+
+    def own(way, q):
+        device = {"tensor": z + (1, -1, 0)[way], "pipe": dest}
+        return pltpu.make_async_remote_copy(
+            src_ref=packed.at[piece(q)],
+            dst_ref=buf.at[place, c, piece(q)],
+            send_sem=own_sem.at[way, q],
+            recv_sem=recv_sem.at[place, c, q],
+            device_id=device,
+            device_id_type=MESH,
+        )
+
+    goes = (z < nz - 1, z > 0, dest != c)
+
+    for q in range(PIECES):
+        for way in range(3):
+
+            @pl.when(goes[way])
+            def _():
+                own(way, q).start()
+
+    @pl.when(dest == c)
+    def _():
+        buf[place, c] = packed[...]
+
+    packed_x = jnp.dot(pick[...], x_in[...], preferred_element_type=jnp.float32).astype(
+        jnp.bfloat16
+    )
+    narrow[:, 0:64] = jnp.dot(packed_x, proj[...], preferred_element_type=jnp.float32)
+    narrow[:, 64:128] = jnp.dot(packed[...], proj[...], preferred_element_type=jnp.float32)
+
+    def passed(j, k, q, step):
+        return pltpu.make_async_remote_copy(
+            src_ref=buf.at[j, k, piece(q)],
+            dst_ref=buf.at[j, k, piece(q)],
+            send_sem=fwd_sem.at[j, k, q],
+            recv_sem=recv_sem.at[j, k, q],
+            device_id={"tensor": z + step, "pipe": c},
+            device_id_type=MESH,
+        )
+
+    def each(do):
+        for q in range(PIECES):
+            for i in range(half):
+                j = c * i + (1 - c) * (half - 1 - i)
+                source = c * half + j
+                for k in range(2):
+                    do(j, k, q, source)
+
+    def receive(j, k, q, source):
+        @pl.when((source != z) | (k != c))
+        def _():
+            passed(j, k, q, 0).wait_recv()
+
+        @pl.when((source < z) & (z < nz - 1))
+        def _():
+            passed(j, k, q, 1).start()
+
+        @pl.when((source > z) & (z > 0))
+        def _():
+            passed(j, k, q, -1).start()
+
+    def finish(j, k, q, source):
+        @pl.when(((source < z) & (z < nz - 1)) | ((source > z) & (z > 0)))
+        def _():
+            passed(j, k, q, 0).wait_send()
+
+    each(receive)
+    for q in range(PIECES):
+        for way in range(3):
+
+            @pl.when(goes[way])
+            def _():
+                own(way, q).wait_send()
+
+    each(finish)
+
+
+def hidden_kernel(tiles, half, buf, weight, gate, up, proj, pick, out, mine, sent, got, send_sem, recv_sem):
+    i = pl.program_id(0)
+    c = lax.axis_index("pipe")
+    width = buf.shape[3]
+
+    def copy(t):
+        return pltpu.make_async_remote_copy(
+            src_ref=sent.at[t],
+            dst_ref=got.at[t],
+            send_sem=send_sem.at[t],
+            recv_sem=recv_sem.at[t],
+            device_id={"pipe": 1 - c},
+            device_id_type=MESH,
+        )
+
+    def part(core):
+        total = None
+        for j in range(half):
+            term = lax.dot_general(
+                buf[j, core],
+                weight[:, j * width : (j + 1) * width],
+                LAST,
+                preferred_element_type=jnp.float32,
+            )
+            total = term if total is None else total + term
+        return total
+
+    @pl.when(i == 0)
+    def _():
+        greet([{"pipe": 1 - c}])
+        out[...] = jnp.zeros_like(out)
+
+    @pl.when(i < tiles)
+    def _():
+        sent[i] = part(1 - c).astype(jnp.bfloat16)
+        copy(i).start()
+        mine[i % 2] = part(c)
+
+    @pl.when(i > 0)
+    def _():
+        t = i - 1
+        gate_val = jnp.dot(pick[...], gate[...], preferred_element_type=jnp.float32)
+        up_val = jnp.dot(pick[...], up[...], preferred_element_type=jnp.float32)
+        sig = jax.nn.sigmoid(gate_val)
+        act = gate_val * sig
+        slope = sig * (1.0 + gate_val * (1.0 - sig))
+        table = proj[...]
+        out[0] += jnp.dot(
+            (act * up_val).astype(jnp.bfloat16), table, preferred_element_type=jnp.float32
+        )
+        copy(t).wait_recv()
+        grad = mine[t % 2] + got[t].astype(jnp.float32)
+        out[1] += jnp.dot(
+            (grad * act).astype(jnp.bfloat16), table, preferred_element_type=jnp.float32
+        )
+        out[2] += jnp.dot(
+            (grad * up_val * slope).astype(jnp.bfloat16),
+            table,
+            preferred_element_type=jnp.float32,
+        )
+
+    @pl.when(i == tiles)
+    def _():
+        @pl.loop(0, tiles)
+        def _(t):
+            copy(t).wait_send()
+
+
+def tensor_sum_kernel(n, part, out, got, send_sem, recv_sem, send2, recv2):
+    me = lax.axis_index("tensor")
+    peers = [lax.rem(me + d, n) for d in range(1, n)]
+    greet([{"tensor": peer} for peer in peers])
+
+    def first(peer, slot):
+        return pltpu.make_async_remote_copy(
+            src_ref=part.at[peer],
+            dst_ref=got.at[slot],
+            send_sem=send_sem.at[peer],
+            recv_sem=recv_sem.at[slot],
+            device_id={"tensor": peer},
+            device_id_type=MESH,
+        )
+
+    def second(peer, slot):
+        return pltpu.make_async_remote_copy(
+            src_ref=out.at[slot],
+            dst_ref=out.at[slot],
+            send_sem=send2.at[peer],
+            recv_sem=recv2.at[slot],
+            device_id={"tensor": peer},
+            device_id_type=MESH,
+        )
+
+    for peer in peers:
+        first(peer, me).start()
+    got[me] = part[me]
+    for peer in peers:
+        first(peer, peer).wait_recv()
+    total = got[0]
+    for k in range(1, n):
+        total = total + got[k]
+    out[me] = total
+    for peer in peers:
+        second(peer, me).start()
+    for peer in peers:
+        second(peer, peer).wait_recv()
+    for peer in peers:
+        first(peer, me).wait_send()
+        second(peer, me).wait_send()
+
+
+def small_sum_kernel(axes, count_axes, *refs):
+    if count_axes:
+        part, count, out, counts, got, send_sem, recv_sem, csend, crecv = refs
+    else:
+        part, out, got, send_sem, recv_sem = refs
+
+    def layout(names):
+        sizes = [lax.axis_size(a) for a in names]
+        me = lax.axis_index(names[0])
+        for name, size in zip(names[1:], sizes[1:]):
+            me = me * size + lax.axis_index(name)
+        n = int(np.prod(sizes))
+        peers = []
+        for d in range(1, n):
+            flat = lax.rem(me + d, n)
+            rest, device = flat, {}
+            for name, size in reversed(list(zip(names, sizes))):
+                device[name] = lax.rem(rest, size)
+                rest = rest // size
+            peers.append((flat, device))
+        return n, me, peers
+
+    n, me, peers = layout(axes)
+
+    def copy(flat, device, slot):
+        return pltpu.make_async_remote_copy(
+            src_ref=part,
+            dst_ref=got.at[slot],
+            send_sem=send_sem.at[flat],
+            recv_sem=recv_sem.at[slot],
+            device_id=device,
+            device_id_type=MESH,
+        )
+
+    if count_axes:
+        cn, cme, cpeers = layout(count_axes)
+
+        def ccopy(flat, device, slot):
+            return pltpu.make_async_remote_copy(
+                src_ref=count,
+                dst_ref=counts.at[slot],
+                send_sem=csend.at[flat],
+                recv_sem=crecv.at[slot],
+                device_id=device,
+                device_id_type=MESH,
+            )
+
+        greet([device for _, device in cpeers])
+    else:
+        greet([device for _, device in peers])
+    for flat, device in peers:
+        copy(flat, device, me).start()
+    if count_axes:
+        for flat, device in cpeers:
+            ccopy(flat, device, cme).start()
+        counts[cme] = count[...]
+    got[me] = part[...]
+    for flat, device in peers:
+        copy(flat, device, flat).wait_recv()
+    total = got[0]
+    for k in range(1, n):
+        total = total + got[k]
+    out[...] = total
+    for flat, device in peers:
+        copy(flat, device, me).wait_send()
+    if count_axes:
+        for flat, device in cpeers:
+            ccopy(flat, device, flat).wait_recv()
+        for flat, device in cpeers:
+            ccopy(flat, device, cme).wait_send()
+
+
+def packed_body(
+    x_in,
+    grad_out,
+    gate_pre,
+    up_pre,
+    w_down,
+    proj_in,
+    proj_ff,
+    resp_mask,
+    doc_lengths,
+    owner,
+    bank_grads,
+):
+    nz, npipe = lax.axis_size("tensor"), lax.axis_size("pipe")
+    half = nz // npipe
+    tokens, width = grad_out.shape
+    hidden_units = gate_pre.shape[1]
+    rank = proj_in.shape[1]
+    tile = 256
+    tiles = hidden_units // tile
+    f32, b16 = jnp.float32, jnp.bfloat16
+    dma = pltpu.SemaphoreType.DMA
+
+    order = jnp.cumsum(resp_mask) - 1
+    taken = jnp.sum(resp_mask)
+    pick = ((order[None, :] == jnp.arange(CAP)[:, None]) & (resp_mask[None, :] > 0)).astype(b16)
+    offset = lax.axis_index(("bank", "pipe")) * tokens
+    positions = offset + jnp.arange(tokens, dtype=jnp.int32)
+    doc_ends = jnp.cumsum(doc_lengths)
+    starts = doc_ends - doc_lengths
+    inside = (positions[:, None] >= starts[None, :]) & (positions[:, None] < doc_ends[None, :])
+    member = jnp.dot(pick, inside.astype(b16), preferred_element_type=f32)
+    nex = doc_lengths.shape[0]
+
+    buf, narrow = pl.pallas_call(
+        functools.partial(gather_kernel, nz, half),
+        out_shape=(
+            jax.ShapeDtypeStruct((half, npipe, CAP, width), b16),
+            jax.ShapeDtypeStruct((CAP, 2 * rank), f32),
+        ),
+        in_specs=[VMEM] * 4,
+        out_specs=(VMEM, VMEM),
+        scratch_shapes=[
+            pltpu.VMEM((CAP, width), b16),
+            dma((3, PIECES)),
+            dma((half, npipe, PIECES)),
+            dma((half, npipe, PIECES)),
+        ],
+        compiler_params=params(0),
+        name="gather",
+    )(pick, grad_out, x_in, proj_in)
+
+    wide = pl.pallas_call(
+        functools.partial(hidden_kernel, tiles, half),
+        grid=(tiles + 1,),
+        out_shape=jax.ShapeDtypeStruct((3, CAP, rank), f32),
+        in_specs=[
+            pl.BlockSpec((half, npipe, CAP, width), lambda i: (0, 0, 0, 0)),
+            pl.BlockSpec((tile, half * width), lambda i: (jnp.minimum(i, tiles - 1), 0)),
+            pl.BlockSpec((tokens, tile), lambda i: (0, jnp.maximum(i - 1, 0))),
+            pl.BlockSpec((tokens, tile), lambda i: (0, jnp.maximum(i - 1, 0))),
+            pl.BlockSpec((tile, rank), lambda i: (jnp.maximum(i - 1, 0), 0)),
+            pl.BlockSpec((CAP, tokens), lambda i: (0, 0)),
+        ],
+        out_specs=pl.BlockSpec((3, CAP, rank), lambda i: (0, 0, 0)),
+        scratch_shapes=[
+            pltpu.VMEM((2, CAP, tile), f32),
+            pltpu.VMEM((tiles, CAP, tile), b16),
+            pltpu.VMEM((tiles, CAP, tile), b16),
+            dma((tiles,)),
+            dma((tiles,)),
+        ],
+        compiler_params=params(1, dimension_semantics=("arbitrary",)),
+        name="hidden",
+    )(buf, w_down, gate_pre, up_pre, proj_ff, pick)
+
+    partials = jnp.concatenate(
+        [wide[0], wide[1], wide[2], narrow, jnp.zeros((CAP, rank), f32)], axis=1
+    ).reshape(nz, CAP // nz, 6 * rank)
+    shape = (nz, CAP // nz, 6 * rank)
+    projected = pl.pallas_call(
+        functools.partial(tensor_sum_kernel, nz),
+        out_shape=jax.ShapeDtypeStruct(shape, f32),
+        in_specs=[VMEM],
+        out_specs=VMEM,
+        scratch_shapes=[pltpu.VMEM(shape, f32)] + [dma((nz,))] * 4,
+        compiler_params=params(2),
+        name="tensor_sum",
+    )(partials).reshape(CAP, 6 * rank)
+
+    a_down, b_wide = projected[:, :rank], projected[:, rank : 3 * rank]
+    a_in, b_down = projected[:, 3 * rank : 4 * rank], projected[:, 4 * rank : 5 * rank]
+
+    def grads(left, right):
+        masked = (member[:, :, None] * left[:, None, :]).reshape(CAP, nex * rank)
+        return lax.dot_general(
+            masked,
+            right,
+            (((0,), (0,)), ((), ())),
+            precision=lax.Precision.HIGHEST,
+            preferred_element_type=f32,
+        ).reshape(nex, rank, right.shape[1])
+
+    first = grads(a_down, b_down)
+    rest = grads(a_in, b_wide)
+    whole = jnp.stack([first, rest[..., :rank], rest[..., rank:]], axis=1).reshape(nex, -1)
+    kron_part = bank_grads.shape[2]
+    mine = lax.dynamic_slice_in_dim(
+        whole, lax.axis_index("tensor") * kron_part, kron_part, axis=1
+    )
+
+    def small_sum(part, axes, cid, count=None, count_axes=None):
+        n = int(np.prod([lax.axis_size(a) for a in axes]))
+        outs = [jax.ShapeDtypeStruct(part.shape, f32)]
+        scratch = [pltpu.VMEM((n,) + part.shape, f32), dma((n,)), dma((n,))]
+        operands = [part]
+        if count_axes:
+            cn = int(np.prod([lax.axis_size(a) for a in count_axes]))
+            outs.append(jax.ShapeDtypeStruct((cn,) + count.shape, f32))
+            scratch += [dma((cn,)), dma((cn,))]
+            operands.append(count)
+        return pl.pallas_call(
+            functools.partial(small_sum_kernel, axes, count_axes),
+            out_shape=tuple(outs),
+            in_specs=[VMEM] * len(operands),
+            out_specs=(VMEM,) * len(outs),
+            scratch_shapes=scratch,
+            compiler_params=params(cid),
+            name="small_sum",
+        )(*operands)
+
+    example_grads, counts = small_sum(
+        mine,
+        ("bank", "pipe"),
+        3,
+        jnp.full((8, 128), taken, f32),
+        ("groups", "bank", "pipe"),
+    )
+    partial_value = lax.dot_general(
+        example_grads,
+        bank_grads[0].astype(f32),
+        LAST,
+        precision=lax.Precision.HIGHEST,
+        preferred_element_type=f32,
+    )
+    owned = (owner == lax.axis_index("bank")).astype(f32)[:, None]
+    (scores,) = small_sum(partial_value * owned, ("tensor", "bank"), 4)
+    return lax.cond(
+        jnp.max(counts) > CAP,
+        lambda: body(
+            x_in,
+            grad_out,
+            gate_pre,
+            up_pre,
+            w_down,
+            proj_in,
+            proj_ff,
+            resp_mask,
+            doc_lengths,
+            owner,
+            bank_grads,
+        ),
+        lambda: scores,
+    )
+
+
+def choose(*args):
+    nz = lax.axis_size("tensor")
+    fits = (
+        lax.axis_size("pipe") == 2
+        and nz % 2 == 0
+        and 2 < nz <= 8
+        and args[0].shape[0] >= CAP
+        and CAP % (8 * nz) == 0
+        and args[0].shape[1] % 128 == 0
+        and args[2].shape[1] % 256 == 0
+        and args[5].shape[1] == 64
+    )
+    return packed_body(*args) if fits else body(*args)
+
+
 def solution(mesh):
     return jax.shard_map(
-        body,
+        choose,
         mesh=mesh,
         in_specs=(
             P(("groups", "bank", "pipe"), "tensor"),

time: 343 us -> 197 us (0.57)
  waiting for transfers between devices: 196 us -> 0 us
  Pallas kernels: 0 us -> 160 us
  matrix products: 50 us -> 6.01 us
  blocking collectives: 34.6 us -> 0 us
  local copies, waits for them, and re-layouts: 39.4 us -> 10.2 us
  other arithmetic: 9.77 us -> 4.94 us
    pallas_call x0 -> x5, Pallas kernels: none -> 160 us  [the longest x1 87.1 us: packed_body(): pl.pallas_call(functools.partial(hidden_kernel, tiles, half), grid=(tiles...]
    all_gather x1 -> x0, waiting for transfers between devices: 101 us -> none  [body(): full_rows = lax.all_gather(grad_out, 'tensor', axis=1, tiled=True)]
    psum x2 -> x0, waiting for transfers between devices: 72.5 us -> none  [the longest x1 41.5 us: body(): projected = lax.psum(partials, 'tensor')]
    dot_general x5 -> x4, matrix products: 50 us -> 6.01 us  [the longest x2 3.55 us: grads(): lax.dot_general(masked, right, (((0,), (0,)), ((), ())), precision=lax.Pr...]
    gather x2 -> x0, local copies, waits for them, and re-layouts: 27.8 us -> none  [the longest x1 14.9 us: body(): jnp.take(stacked, left_ids, axis=0) * jnp.take(stacked, right_ids, axis=0)]
    reduce_scatter x1 -> x0, waiting for transfers between devices: 22.1 us -> none  [body(): lax.psum_scatter(lax.dot_general(paired, w_down, contract_last, preferred...]
    psum x1 -> x0, blocking collectives: 21 us -> none  [body(): scores = lax.psum(partial_value * owned, ('tensor', 'bank'))]
    all_to_all x1 -> x0, blocking collectives: 13.6 us -> none  [body(): lax.all_to_all(full_rows, 'pipe', split_axis=1, concat_axis=0, tiled=True)]
  transfers between devices with their start and end apart: 4 -> 0, of which waited for: 4 -> 0; matrix products, arithmetic and copies ran while one was open for 1% -> 0% of each run, Pallas kernels for 0% -> 0%
where the time goes in v1:
time: 197 us; the launch traced here: 196 us
  Pallas kernels  160 us (81%)
  between operations  14.9 us (8%)
  local copies, waits for them, and re-layouts  10.2 us (5%)
  matrix products  6.01 us (3%)
  other arithmetic  4.94 us (3%)
    pallas_call x1, Pallas kernels, packed_body(): pl.pallas_call(functools.partial(hidden_kernel, tiles, half), grid=(tiles...  87.1 us
    pallas_call x1, Pallas kernels, packed_body(): pl.pallas_call(functools.partial(gather_kernel, nz, half), out_shape=(jax...  27.6 us
    pallas_call x1, Pallas kernels, packed_body(): pl.pallas_call(functools.partial(tensor_sum_kernel, nz), out_shape=jax.Sh...  24.7 us
    pallas_call x2, Pallas kernels, small_sum(): pl.pallas_call(functools.partial(small_sum_kernel, axes, count_axes), out...  20.6 us
    unnamed x15, local copies, waits for them, and re-layouts  4.7 us

profile of v1, /device:TPU:0, one launch (start us, length us, event | category | flops | bytes accessed | tf_op | source)
XLA Modules:
  0.0 196.3 jit_solution(6719209287178379130)
XLA Ops:
  6.5 1.0 reduce-window.27
  7.8 0.7 broadcast_compare_fusion
  8.5 0.9 fusion.63.pick
  9.4 1.8 copy.40.proj
  11.2 27.6 %gather.11 = (bf16[2,2,320,1280]{3,2,1,0:T(8,128)(2,1)}, f32[320,128]{1,0:T(8,128)}) custom-call(bf16[320,512]{1,0:T(8,128)(2,1)} %fusion.63.pick, bf16[512,1280]{1,0:T(8,128)(2,1)} %grad.1, bf16[512,1280]{1,0:T(8,128)(2,1)} %x_in.1, bf16[1280,64]{1,0:T(8,128)(2,1)} %copy.40.proj), custom_call_target="tpu_custom_call" | custom-call | tf_op jit(solution)/shard_map/gather/pallas_call | solution.py:433
  38.8 2.3 %copy.41.proj = bf16[4352,64]{1,0:T(8,128)(2,1)} copy(bf16[4352,64]{0,1:T(8,128)(2,1)} %param.23) | data formatting | bytes 1114112 | tf_op args[6]
  41.1 87.1 %hidden.1 = f32[3,320,64]{2,1,0:T(8,128)} custom-call(bf16[2,2,320,1280]{3,2,1,0:T(8,128)(2,1)} %get-tuple-element.53.buf, bf16[4352,2560]{1,0:T(8,128)(2,1)} %weight.1, bf16[512,4352]{1,0:T(8,128)(2,1)} %gate.1, bf16[512,4352]{1,0:T(8,128)(2,1)} %up.1, bf16[4352,64]{1,0:T(8,128)(2,1)} %copy.41.proj, bf16[320,512]{1,0:T(8,128)(2,1)} %fusion.63.pick), custom_call_target="tpu_custom_call" | custom-call | tf_op jit(solution)/shard_map/hidden/pallas_call | solution.py:451
  128.3 1.3 fusion.79
  129.6 1.0 concatenate.19.part
  130.6 24.7 %tensor_sum.1 = f32[4,80,384]{2,1,0:T(8,128)} custom-call(f32[4,80,384]{2,1,0:T(8,128)} %concatenate.19.part), custom_call_target="tpu_custom_call" | custom-call | tf_op jit(solution)/shard_map/tensor_sum/pallas_call | solution.py:479
  155.3 1.1 fusion.78
  156.7 0.2 fusion.64
  156.9 1.7 convolution_bitcast_fusion
  158.8 1.8 fusion.56
  160.9 0.3 reshape.138
  161.2 0.6 constant_dynamic-slice_fusion.refs_0_
  161.9 0.6 reduce_sum.9
  163.2 0.6 broadcast_in_dim.11.refs_1_
  163.7 10.3 %small_sum.2 = (f32[8,3072]{1,0:T(8,128)}, f32[8,8,128]{2,1,0:T(8,128)}) custom-call(f32[8,3072]{1,0:T(8,128)} %constant_dynamic-slice_fusion.refs_0_, f32[8,128]{1,0:T(8,128)} %broadcast_in_dim.11.refs_1_), custom_call_target="tpu_custom_call" | custom-call | tf_op jit(solution)/shard_map/small_sum/pallas_call | solution.py:520
  174.1 2.2 %convolution_multiply_fusion.1.refs_0_ = f32[8,128]{1,0:T(8,128)} fusion(f32[8,3072]{1,0:T(8,128)} %get-tuple-element.56, bf16[1,128,3072]{2,1,0:T(8,128)(2,1)S(1)} %copy-done.2, f32[8]{0:T(128)S(1)} %compare_convert_fusion.1), kind=kOutput, calls=%fused_computation.69 | convolution fusion | flops 37749760 | bytes 888864 | tf_op jit(solution)/shard_map/dot_general | solution.py:537
  176.3 10.3 %small_sum.3 = f32[8,128]{1,0:T(8,128)S(1)} custom-call(f32[8,128]{1,0:T(8,128)} %convolution_multiply_fusion.1.refs_0_), custom_call_target="tpu_custom_call" | custom-call | tf_op jit(solution)/shard_map/small_sum/pallas_call | solution.py:520
  186.6 1.4 reduce_max.9
  188.6 0.2 conditional.1
  188.9 0.6 copy.52
  (26 shorter events, 1.1 us)
Async XLA Ops:
  41.1 88.5 %copy-start.4 = (f32[320,128]{1,0:T(8,128)S(1)}, f32[320,128]{1,0:T(8,128)}, u32[]{:S(2)}) copy-start(f32[320,128]{1,0:T(8,128)} %get-tuple-element.54) | copy-start | bytes 491524
  41.1 115.4 %copy-start.9 = (s32[8]{0:T(128)S(1)}, s32[8]{0:T(128)}, u32[]{:S(2)}) copy-start(s32[8]{0:T(128)} %param.25) | copy-start | bytes 100
  128.2 33.6 %copy-start.6 = (s32[512]{0:T(512)S(1)}, s32[512]{0:T(512)}, u32[]{:S(2)}) copy-start(s32[512]{0:T(512)} %param.24) | copy-start | bytes 6148
  128.3 45.8 %copy-start.10 = (s32[8]{0:T(128)S(1)}, s32[8]{0:T(128)}, u32[]{:S(2)}) copy-start(s32[8]{0:T(128)} %param.26) | copy-start | bytes 100
  128.3 45.8 %copy-start.2 = (bf16[1,128,3072]{2,1,0:T(8,128)(2,1)S(1)}, bf16[1,128,3072]{2,1,0:T(8,128)(2,1)}, u32[]{:S(2)}) copy-start(bf16[1,128,3072]{2,1,0:T(8,128)(2,1)} %param.27) | copy-start | bytes 2359300
  128.3 60.3 %copy-start.1 = (bf16[512,1280]{1,0:T(8,128)(2,1)S(1)}, bf16[512,1280]{1,0:T(8,128)(2,1)}, u32[]{:S(2)}) copy-start(bf16[512,1280]{1,0:T(8,128)(2,1)} %grad.1) | copy-start | bytes 3932164

commit v2 on v1

--- a/solution.py
+++ b/solution.py
@@ -11,7 +11,7 @@
 VMEM = pl.BlockSpec(memory_space=pltpu.VMEM)
 CAP = 320
 PIECES = 4
-LIMIT = 56 * 1024 * 1024
+LIMIT = 60 * 1024 * 1024
 LAST = (((1,), (1,)), ((), ()))
 
 
@@ -108,11 +108,48 @@
     pl.semaphore_wait(barrier, len(devices))
 
 
-def gather_kernel(nz, half, pick, grad, x_in, proj, buf, narrow, packed, own_sem, fwd_sem, recv_sem):
+def layer_kernel(
+    nz,
+    half,
+    tiles,
+    tile,
+    pick,
+    grad,
+    x_in,
+    proj_in,
+    proj_ff,
+    weight,
+    gate,
+    up,
+    wide,
+    narrow,
+    buf,
+    packed,
+    held,
+    gate_in,
+    up_in,
+    act,
+    rate,
+    mine,
+    sent,
+    got,
+    own_sem,
+    fwd_sem,
+    recv_sem,
+    held_sem,
+    gate_sem,
+    up_sem,
+    send_sem,
+    got_sem,
+):
     z, c = lax.axis_index("tensor"), lax.axis_index("pipe")
     other = 1 - c
     dest, place = z // half, z % half
+    rank = proj_in.shape[0]
+    width = packed.shape[1]
     rows = packed.shape[0] // PIECES
+    part_rows = packed.shape[0] // 2
+    events = 2 * half
     barrier = pltpu.get_barrier_semaphore()
     pl.semaphore_signal(barrier, inc=1, device_id={"pipe": other}, device_id_type=MESH)
     for step in (-1, 1):
@@ -127,23 +164,34 @@
                     device_id_type=MESH,
                 )
 
-    inner = jnp.where((z > 0) & (z < nz - 1), 5, 3)
+    def columns(t):
+        return pl.ds(pl.multiple_of(t * tile, tile), tile)
+
+    def hold(t):
+        return pltpu.make_async_copy(weight.at[columns(t)], held.at[t], held_sem.at[t])
+
+    def fetch(t, do):
+        slot = t % 2
+        do(pltpu.make_async_copy(gate.at[:, columns(t)], gate_in.at[slot], gate_sem.at[slot]))
+        do(pltpu.make_async_copy(up.at[:, columns(t)], up_in.at[slot], up_sem.at[slot]))
+
+    fetch(0, lambda d: d.start())
+    fetch(1, lambda d: d.start())
     packed[...] = jnp.dot(pick[...], grad[...], preferred_element_type=jnp.float32).astype(
         jnp.bfloat16
     )
-    pl.semaphore_wait(barrier, inner)
+    pl.semaphore_wait(barrier, jnp.where((z > 0) & (z < nz - 1), 5, 3))
 
     def piece(q):
-        return pl.ds(q * rows, rows)
+        return pl.ds(pl.multiple_of(q * rows, 16), rows)
 
     def own(way, q):
-        device = {"tensor": z + (1, -1, 0)[way], "pipe": dest}
         return pltpu.make_async_remote_copy(
             src_ref=packed.at[piece(q)],
             dst_ref=buf.at[place, c, piece(q)],
             send_sem=own_sem.at[way, q],
             recv_sem=recv_sem.at[place, c, q],
-            device_id=device,
+            device_id={"tensor": z + (1, -1, 0)[way], "pipe": dest},
             device_id_type=MESH,
         )
 
@@ -156,6 +204,10 @@
             def _():
                 own(way, q).start()
 
+    @pl.loop(0, tiles)
+    def _(t):
+        hold(t).start()
+
     @pl.when(dest == c)
     def _():
         buf[place, c] = packed[...]
@@ -163,8 +215,13 @@
     packed_x = jnp.dot(pick[...], x_in[...], preferred_element_type=jnp.float32).astype(
         jnp.bfloat16
     )
-    narrow[:, 0:64] = jnp.dot(packed_x, proj[...], preferred_element_type=jnp.float32)
-    narrow[:, 64:128] = jnp.dot(packed[...], proj[...], preferred_element_type=jnp.float32)
+    narrow[:, 0:rank] = lax.dot_general(
+        packed_x, proj_in[...], LAST, preferred_element_type=jnp.float32
+    )
+    narrow[:, rank : 2 * rank] = lax.dot_general(
+        packed[...], proj_in[...], LAST, preferred_element_type=jnp.float32
+    )
+    wide[...] = jnp.zeros_like(wide)
 
     def passed(j, k, q, step):
         return pltpu.make_async_remote_copy(
@@ -176,15 +233,14 @@
             device_id_type=MESH,
         )
 
-    def each(do):
-        for q in range(PIECES):
-            for i in range(half):
-                j = c * i + (1 - c) * (half - 1 - i)
-                source = c * half + j
-                for k in range(2):
-                    do(j, k, q, source)
-
-    def receive(j, k, q, source):
+    def event(e):
+        q, i, k = e // events, (e // 2) % half, e % 2
+        j = c * i + (1 - c) * (half - 1 - i)
+        return j, k, q, c * half + j
+
+    def receive(e):
+        j, k, q, source = event(e)
+
         @pl.when((source != z) | (k != c))
         def _():
             passed(j, k, q, 0).wait_recv()
@@ -197,88 +253,122 @@
         def _():
             passed(j, k, q, -1).start()
 
-    def finish(j, k, q, source):
-        @pl.when(((source < z) & (z < nz - 1)) | ((source > z) & (z > 0)))
-        def _():
-            passed(j, k, q, 0).wait_send()
-
-    each(receive)
-    for q in range(PIECES):
-        for way in range(3):
-
-            @pl.when(goes[way])
-            def _():
-                own(way, q).wait_send()
-
-    each(finish)
-
-
-def hidden_kernel(tiles, half, buf, weight, gate, up, proj, pick, out, mine, sent, got, send_sem, recv_sem):
-    i = pl.program_id(0)
-    c = lax.axis_index("pipe")
-    width = buf.shape[3]
-
-    def copy(t):
+    @pl.loop(0, tiles)
+    def _(t):
+        slot = t % 2
+        fetch(t, lambda d: d.wait())
+        gate_val = jnp.dot(pick[...], gate_in[slot], preferred_element_type=jnp.float32)
+        up_val = jnp.dot(pick[...], up_in[slot], preferred_element_type=jnp.float32)
+
+        @pl.when(t + 2 < tiles)
+        def _():
+            fetch(t + 2, lambda d: d.start())
+
+        sig = jax.nn.sigmoid(gate_val)
+        silu = gate_val * sig
+        act[t] = silu
+        rate[t] = up_val * (sig * (1.0 + gate_val * (1.0 - sig)))
+        wide[0] += lax.dot_general(
+            (silu * up_val).astype(jnp.bfloat16),
+            proj_ff[:, columns(t)],
+            LAST,
+            preferred_element_type=jnp.float32,
+        )
+
+        @pl.when((t % 4 == 3) & (t // 4 < events))
+        def _():
+            receive(t // 4)
+
+    early = min(events, tiles // 4)
+    middle = events * PIECES // 2
+
+    @pl.loop(early, middle)
+    def _(e):
+        receive(e)
+
+    def copy(s):
         return pltpu.make_async_remote_copy(
-            src_ref=sent.at[t],
-            dst_ref=got.at[t],
-            send_sem=send_sem.at[t],
-            recv_sem=recv_sem.at[t],
-            device_id={"pipe": 1 - c},
+            src_ref=sent.at[s],
+            dst_ref=got.at[s],
+            send_sem=send_sem.at[s],
+            recv_sem=got_sem.at[s],
+            device_id={"pipe": other},
             device_id_type=MESH,
         )
 
-    def part(core):
+    def rows_of(s):
+        return pl.ds(pl.multiple_of((s // tiles) * part_rows, 16), part_rows)
+
+    def multiply(s):
+        t, these = s % tiles, rows_of(s)
         total = None
         for j in range(half):
+            left = jnp.concatenate([buf[j, other, these], buf[j, c, these]], axis=0)
             term = lax.dot_general(
-                buf[j, core],
-                weight[:, j * width : (j + 1) * width],
+                left,
+                held[t, :, j * width : (j + 1) * width],
                 LAST,
                 preferred_element_type=jnp.float32,
             )
             total = term if total is None else total + term
-        return total
-
-    @pl.when(i == 0)
-    def _():
-        greet([{"pipe": 1 - c}])
-        out[...] = jnp.zeros_like(out)
-
-    @pl.when(i < tiles)
-    def _():
-        sent[i] = part(1 - c).astype(jnp.bfloat16)
-        copy(i).start()
-        mine[i % 2] = part(c)
-
-    @pl.when(i > 0)
-    def _():
-        t = i - 1
-        gate_val = jnp.dot(pick[...], gate[...], preferred_element_type=jnp.float32)
-        up_val = jnp.dot(pick[...], up[...], preferred_element_type=jnp.float32)
-        sig = jax.nn.sigmoid(gate_val)
-        act = gate_val * sig
-        slope = sig * (1.0 + gate_val * (1.0 - sig))
-        table = proj[...]
-        out[0] += jnp.dot(
-            (act * up_val).astype(jnp.bfloat16), table, preferred_element_type=jnp.float32
-        )
-        copy(t).wait_recv()
-        grad = mine[t % 2] + got[t].astype(jnp.float32)
-        out[1] += jnp.dot(
-            (grad * act).astype(jnp.bfloat16), table, preferred_element_type=jnp.float32
-        )
-        out[2] += jnp.dot(
-            (grad * up_val * slope).astype(jnp.bfloat16),
-            table,
-            preferred_element_type=jnp.float32,
-        )
-
-    @pl.when(i == tiles)
-    def _():
-        @pl.loop(0, tiles)
-        def _(t):
-            copy(t).wait_send()
+        sent[s] = total[:part_rows].astype(jnp.bfloat16)
+        copy(s).start()
+        mine[s % 2] = total[part_rows:]
+
+    def finish(s):
+        t, these = s % tiles, rows_of(s)
+        copy(s).wait_recv()
+        hidden_grad = mine[s % 2] + got[s].astype(jnp.float32)
+        table = proj_ff[:, columns(t)]
+        for index, factor in ((1, act), (2, rate)):
+            wide[index, these] += lax.dot_general(
+                (hidden_grad * factor[t, these]).astype(jnp.bfloat16),
+                table,
+                LAST,
+                preferred_element_type=jnp.float32,
+            )
+
+    @pl.loop(0, tiles)
+    def _(s):
+        hold(s).wait()
+        multiply(s)
+
+        @pl.when(s > 0)
+        def _():
+            finish(s - 1)
+
+        @pl.when((s % 2 == 1) & (s // 2 < middle))
+        def _():
+            receive(middle + s // 2)
+
+    for e in range(tiles // 2, middle):
+        receive(middle + e)
+
+    @pl.loop(tiles, 2 * tiles)
+    def _(s):
+        multiply(s)
+        finish(s - 1)
+
+    finish(2 * tiles - 1)
+
+    @pl.loop(0, 2 * tiles)
+    def _(s):
+        copy(s).wait_send()
+
+    for q in range(PIECES):
+        for way in range(3):
+
+            @pl.when(goes[way])
+            def _():
+                own(way, q).wait_send()
+
+    @pl.loop(0, events * PIECES)
+    def _(e):
+        j, k, q, source = event(e)
+
+        @pl.when(((source < z) & (z < nz - 1)) | ((source > z) & (z > 0)))
+        def _():
+            passed(j, k, q, 0).wait_send()
 
 
 def tensor_sum_kernel(n, part, out, got, send_sem, recv_sem, send2, recv2):
@@ -430,47 +520,38 @@
     member = jnp.dot(pick, inside.astype(b16), preferred_element_type=f32)
     nex = doc_lengths.shape[0]
 
-    buf, narrow = pl.pallas_call(
-        functools.partial(gather_kernel, nz, half),
+    any_place = pl.BlockSpec(memory_space=pl.ANY)
+    wide, narrow = pl.pallas_call(
+        functools.partial(layer_kernel, nz, half, tiles, tile),
         out_shape=(
-            jax.ShapeDtypeStruct((half, npipe, CAP, width), b16),
+            jax.ShapeDtypeStruct((3, CAP, rank), f32),
             jax.ShapeDtypeStruct((CAP, 2 * rank), f32),
         ),
-        in_specs=[VMEM] * 4,
+        in_specs=[VMEM] * 5 + [any_place] * 3,
         out_specs=(VMEM, VMEM),
         scratch_shapes=[
+            pltpu.VMEM((half, npipe, CAP, width), b16),
             pltpu.VMEM((CAP, width), b16),
+            pltpu.VMEM((tiles, tile, half * width), b16),
+            pltpu.VMEM((2, tokens, tile), b16),
+            pltpu.VMEM((2, tokens, tile), b16),
+            pltpu.VMEM((tiles, CAP, tile), f32),
+            pltpu.VMEM((tiles, CAP, tile), f32),
+            pltpu.VMEM((2, CAP // 2, tile), f32),
+            pltpu.VMEM((2 * tiles, CAP // 2, tile), b16),
+            pltpu.VMEM((2 * tiles, CAP // 2, tile), b16),
             dma((3, PIECES)),
             dma((half, npipe, PIECES)),
             dma((half, npipe, PIECES)),
+            dma((tiles,)),
+            dma((2,)),
+            dma((2,)),
+            dma((2 * tiles,)),
+            dma((2 * tiles,)),
         ],
         compiler_params=params(0),
-        name="gather",
-    )(pick, grad_out, x_in, proj_in)
-
-    wide = pl.pallas_call(
-        functools.partial(hidden_kernel, tiles, half),
-        grid=(tiles + 1,),
-        out_shape=jax.ShapeDtypeStruct((3, CAP, rank), f32),
-        in_specs=[
-            pl.BlockSpec((half, npipe, CAP, width), lambda i: (0, 0, 0, 0)),
-            pl.BlockSpec((tile, half * width), lambda i: (jnp.minimum(i, tiles - 1), 0)),
-            pl.BlockSpec((tokens, tile), lambda i: (0, jnp.maximum(i - 1, 0))),
-            pl.BlockSpec((tokens, tile), lambda i: (0, jnp.maximum(i - 1, 0))),
-            pl.BlockSpec((tile, rank), lambda i: (jnp.maximum(i - 1, 0), 0)),
-            pl.BlockSpec((CAP, tokens), lambda i: (0, 0)),
-        ],
-        out_specs=pl.BlockSpec((3, CAP, rank), lambda i: (0, 0, 0)),
-        scratch_shapes=[
-            pltpu.VMEM((2, CAP, tile), f32),
-            pltpu.VMEM((tiles, CAP, tile), b16),
-            pltpu.VMEM((tiles, CAP, tile), b16),
-            dma((tiles,)),
-            dma((tiles,)),
-        ],
-        compiler_params=params(1, dimension_semantics=("arbitrary",)),
-        name="hidden",
-    )(buf, w_down, gate_pre, up_pre, proj_ff, pick)
+        name="layer",
+    )(pick, grad_out, x_in, proj_in.T, proj_ff.T, w_down, gate_pre, up_pre)
 
     partials = jnp.concatenate(
         [wide[0], wide[1], wide[2], narrow, jnp.zeros((CAP, rank), f32)], axis=1

time: 197 us -> 169 us (0.86)
  Pallas kernels: 160 us -> 135 us
  local copies, waits for them, and re-layouts: 10.2 us -> 7.05 us
    pallas_call x2 -> x1, Pallas kernels: 115 us -> 90.3 us  [packed_body(): pl.pallas_call(functools.partial(layer_kernel, nz, half, tiles, tile), ou...]
    unnamed x15 -> x11, local copies, waits for them, and re-layouts: 4.7 us -> 0.62 us
where the time goes in v2:
time: 169 us; the launch traced here: 168 us
  Pallas kernels  135 us (80%)
  between operations  14.9 us (9%)
  local copies, waits for them, and re-layouts  7.05 us (4%)
  matrix products  6.02 us (4%)
  other arithmetic  4.89 us (3%)
    pallas_call x1, Pallas kernels, packed_body(): pl.pallas_call(functools.partial(layer_kernel, nz, half, tiles, tile), ou...  90.3 us
    pallas_call x1, Pallas kernels, packed_body(): pl.pallas_call(functools.partial(tensor_sum_kernel, nz), out_shape=jax.Sh...  24.5 us
    pallas_call x2, Pallas kernels, small_sum(): pl.pallas_call(functools.partial(small_sum_kernel, axes, count_axes), out...  20 us
    dot_general x2, matrix products, grads(): lax.dot_general(masked, right, (((0,), (0,)), ((), ())), precision=lax.Pr...  3.57 us

profile of v2, /device:TPU:0, one launch (start us, length us, event | category | flops | bytes accessed | tf_op | source)
XLA Modules:
  0.0 167.9 jit_solution(12406748395742314990)
XLA Ops:
  6.5 1.0 reduce-window.27
  7.6 0.1 slice_reduce_fusion
  7.8 0.7 broadcast_compare_fusion
  8.5 0.8 fusion.63.pick
  9.3 90.3 %layer.1 = (f32[3,320,64]{2,1,0:T(8,128)}, f32[320,128]{1,0:T(8,128)}) custom-call(bf16[320,512]{1,0:T(8,128)(2,1)} %fusion.63.pick, bf16[512,1280]{1,0:T(8,128)(2,1)} %grad.1, bf16[512,1280]{1,0:T(8,128)(2,1)} %x_in.1, bf16[64,1280]{1,0:T(8,128)(2,1)} %bitcast.91, bf16[64,4352]{1,0:T(8,128)(2,1)} %bitcast.89, bf16[4352,2560]{1,0:T(8,128)(2,1)} %weight.1, ...), custom_call_target="tpu_custom_call" | custom-call | tf_op jit(solution)/shard_map/layer/pallas_call | solution.py:524
  99.7 1.3 fusion.79
  101.0 1.9 %concatenate.19.part = f32[4,80,384]{2,1,0:T(8,128)} concatenate(f32[4,80,64]{2,1,0:T(8,128)S(1)} %bitcast.88, f32[4,80,64]{2,1,0:T(8,128)S(1)} %bitcast.87, f32[4,80,64]{2,1,0:T(8,128)S(1)} %bitcast.86, f32[4,80,128]{2,1,0:T(8,128)} %bitcast.90, f32[4,80,64]{2,1,0:T(8,128)S(1)} %broadcast_in_dim.10), dimensions={2} | concatenate | bytes 983040 | tf_op jit(solution)/shard_map/concatenate | solution.py:556
  102.9 24.5 %tensor_sum.1 = f32[4,80,384]{2,1,0:T(8,128)} custom-call(f32[4,80,384]{2,1,0:T(8,128)} %concatenate.19.part), custom_call_target="tpu_custom_call" | custom-call | tf_op jit(solution)/shard_map/tensor_sum/pallas_call | solution.py:560
  127.4 1.1 fusion.78
  128.7 0.2 reduce-window.29
  128.8 0.2 fusion.64
  129.1 1.8 %fusion.56 = f32[8,64,128]{2,1,0:T(8,128)S(1)} fusion(f32[320,64]{0,1:T(8,128)S(1)} %copy.36, f32[320,8]{0,1:T(8,128)S(1)} %fusion.64, f32[320,384]{1,0:T(8,128)} %bitcast.82), kind=kOutput, calls=%fused_computation.71 | convolution fusion | flops 251822080 | bytes 518144 | tf_op jit(solution)/shard_map/dot_general | solution.py:575
  130.9 0.1 slice_bitcast_fusion.1
  131.2 1.7 %convolution_bitcast_fusion = f32[8,1,64,64]{3,2,0,1:T(8,128)S(1)} fusion(f32[320,64]{0,1:T(8,128)S(1)} %copy.34, f32[320,8]{0,1:T(8,128)S(1)} %fusion.64, f32[320,384]{1,0:T(8,128)} %bitcast.83), kind=kOutput, calls=%fused_computation.68 | convolution fusion | flops 125992960 | bytes 387072 | tf_op jit(solution)/shard_map/dot_general | solution.py:575
  133.1 0.3 reshape.138
  133.4 0.6 constant_dynamic-slice_fusion.refs_0_
  134.0 0.6 reduce_sum.9
  135.3 0.6 broadcast_in_dim.11.refs_1_
  135.9 10.3 %small_sum.2 = (f32[8,3072]{1,0:T(8,128)}, f32[8,8,128]{2,1,0:T(8,128)}) custom-call(f32[8,3072]{1,0:T(8,128)} %constant_dynamic-slice_fusion.refs_0_, f32[8,128]{1,0:T(8,128)} %broadcast_in_dim.11.refs_1_), custom_call_target="tpu_custom_call" | custom-call | tf_op jit(solution)/shard_map/small_sum/pallas_call | solution.py:601
  146.2 2.2 %convolution_multiply_fusion.1.refs_0_ = f32[8,128]{1,0:T(8,128)} fusion(f32[8,3072]{1,0:T(8,128)} %get-tuple-element.56, bf16[1,128,3072]{2,1,0:T(8,128)(2,1)S(1)} %copy-done.2, f32[8]{0:T(128)S(1)} %compare_convert_fusion.1), kind=kOutput, calls=%fused_computation.69 | convolution fusion | flops 37749760 | bytes 888864 | tf_op jit(solution)/shard_map/dot_general | solution.py:618
  148.5 9.7 %small_sum.3 = f32[8,128]{1,0:T(8,128)S(1)} custom-call(f32[8,128]{1,0:T(8,128)} %convolution_multiply_fusion.1.refs_0_), custom_call_target="tpu_custom_call" | custom-call | tf_op jit(solution)/shard_map/small_sum/pallas_call | solution.py:601
  158.2 1.4 reduce_max.9
  160.2 0.2 conditional.1
  160.5 0.6 copy.44
  (21 shorter events, 0.6 us)
Async XLA Ops:
  9.3 119.3 %copy-start.8 = (s32[8]{0:T(128)S(1)}, s32[8]{0:T(128)}, u32[]{:S(2)}) copy-start(s32[8]{0:T(128)} %param.25) | copy-start | bytes 100
  99.7 34.3 %copy-start.5 = (s32[512]{0:T(512)S(1)}, s32[512]{0:T(512)}, u32[]{:S(2)}) copy-start(s32[512]{0:T(512)} %param.24) | copy-start | bytes 6148
  99.7 46.5 %copy-start.9 = (s32[8]{0:T(128)S(1)}, s32[8]{0:T(128)}, u32[]{:S(2)}) copy-start(s32[8]{0:T(128)} %param.26) | copy-start | bytes 100
  99.7 46.5 %copy-start.2 = (bf16[1,128,3072]{2,1,0:T(8,128)(2,1)S(1)}, bf16[1,128,3072]{2,1,0:T(8,128)(2,1)}, u32[]{:S(2)}) copy-start(bf16[1,128,3072]{2,1,0:T(8,128)(2,1)} %param.27) | copy-start | bytes 2359300
  99.7 60.5 %copy-start.1 = (bf16[512,1280]{1,0:T(8,128)(2,1)S(1)}, bf16[512,1280]{1,0:T(8,128)(2,1)}, u32[]{:S(2)}) copy-start(bf16[512,1280]{1,0:T(8,128)(2,1)} %grad.1) | copy-start | bytes 3932164

commit v3 on v2

--- a/solution.py
+++ b/solution.py
@@ -11,6 +11,7 @@
 VMEM = pl.BlockSpec(memory_space=pltpu.VMEM)
 CAP = 320
 PIECES = 4
+LAG = 4
 LIMIT = 60 * 1024 * 1024
 LAST = (((1,), (1,)), ((), ()))
 
@@ -121,6 +122,7 @@
     weight,
     gate,
     up,
+    part,
     wide,
     narrow,
     buf,
@@ -313,12 +315,12 @@
             total = term if total is None else total + term
         sent[s] = total[:part_rows].astype(jnp.bfloat16)
         copy(s).start()
-        mine[s % 2] = total[part_rows:]
+        mine[s % (2 * LAG)] = total[part_rows:]
 
     def finish(s):
         t, these = s % tiles, rows_of(s)
         copy(s).wait_recv()
-        hidden_grad = mine[s % 2] + got[s].astype(jnp.float32)
+        hidden_grad = mine[s % (2 * LAG)] + got[s].astype(jnp.float32)
         table = proj_ff[:, columns(t)]
         for index, factor in ((1, act), (2, rate)):
             wide[index, these] += lax.dot_general(
@@ -333,9 +335,9 @@
         hold(s).wait()
         multiply(s)
 
-        @pl.when(s > 0)
-        def _():
-            finish(s - 1)
+        @pl.when(s >= LAG)
+        def _():
+            finish(s - LAG)
 
         @pl.when((s % 2 == 1) & (s // 2 < middle))
         def _():
@@ -347,9 +349,21 @@
     @pl.loop(tiles, 2 * tiles)
     def _(s):
         multiply(s)
-        finish(s - 1)
-
-    finish(2 * tiles - 1)
+        finish(s - LAG)
+
+    @pl.loop(2 * tiles - LAG, 2 * tiles)
+    def _(s):
+        finish(s)
+
+    block = packed.shape[0] // nz
+    for k in range(nz):
+        low, mid, high = k * block, k * block + block // 2, (k + 1) * block
+        part[k, 0:block, 0:rank] = wide[0, low:high]
+        part[k, 0:block, rank:] = wide[1, low:high]
+        part[k, block : 2 * block, 0:rank] = wide[2, low:high]
+        part[k, block : 2 * block, rank:] = narrow[low:high, 0:rank]
+        part[k, 2 * block :, 0:rank] = narrow[low:mid, rank:]
+        part[k, 2 * block :, rank:] = narrow[mid:high, rank:]
 
     @pl.loop(0, 2 * tiles)
     def _(s):
@@ -521,15 +535,15 @@
     nex = doc_lengths.shape[0]
 
     any_place = pl.BlockSpec(memory_space=pl.ANY)
-    wide, narrow = pl.pallas_call(
+    shape = (nz, 5 * CAP // (2 * nz), 2 * rank)
+    partials = pl.pallas_call(
         functools.partial(layer_kernel, nz, half, tiles, tile),
-        out_shape=(
-            jax.ShapeDtypeStruct((3, CAP, rank), f32),
-            jax.ShapeDtypeStruct((CAP, 2 * rank), f32),
-        ),
+        out_shape=jax.ShapeDtypeStruct(shape, f32),
         in_specs=[VMEM] * 5 + [any_place] * 3,
-        out_specs=(VMEM, VMEM),
+        out_specs=VMEM,
         scratch_shapes=[
+            pltpu.VMEM((3, CAP, rank), f32),
+            pltpu.VMEM((CAP, 2 * rank), f32),
             pltpu.VMEM((half, npipe, CAP, width), b16),
             pltpu.VMEM((CAP, width), b16),
             pltpu.VMEM((tiles, tile, half * width), b16),
@@ -537,7 +551,7 @@
             pltpu.VMEM((2, tokens, tile), b16),
             pltpu.VMEM((tiles, CAP, tile), f32),
             pltpu.VMEM((tiles, CAP, tile), f32),
-            pltpu.VMEM((2, CAP // 2, tile), f32),
+            pltpu.VMEM((2 * LAG, CAP // 2, tile), f32),
             pltpu.VMEM((2 * tiles, CAP // 2, tile), b16),
             pltpu.VMEM((2 * tiles, CAP // 2, tile), b16),
             dma((3, PIECES)),
@@ -553,10 +567,6 @@
         name="layer",
     )(pick, grad_out, x_in, proj_in.T, proj_ff.T, w_down, gate_pre, up_pre)
 
-    partials = jnp.concatenate(
-        [wide[0], wide[1], wide[2], narrow, jnp.zeros((CAP, rank), f32)], axis=1
-    ).reshape(nz, CAP // nz, 6 * rank)
-    shape = (nz, CAP // nz, 6 * rank)
     projected = pl.pallas_call(
         functools.partial(tensor_sum_kernel, nz),
         out_shape=jax.ShapeDtypeStruct(shape, f32),
@@ -565,10 +575,17 @@
         scratch_shapes=[pltpu.VMEM(shape, f32)] + [dma((nz,))] * 4,
         compiler_params=params(2),
         name="tensor_sum",
-    )(partials).reshape(CAP, 6 * rank)
-
-    a_down, b_wide = projected[:, :rank], projected[:, rank : 3 * rank]
-    a_in, b_down = projected[:, 3 * rank : 4 * rank], projected[:, 4 * rank : 5 * rank]
+    )(partials)
+
+    block = CAP // nz
+    a_down = projected[:, :block, :rank].reshape(CAP, rank)
+    b_up = projected[:, :block, rank:]
+    b_gate = projected[:, block : 2 * block, :rank]
+    b_wide = jnp.concatenate([b_up, b_gate], axis=2).reshape(CAP, 2 * rank)
+    a_in = projected[:, block : 2 * block, rank:].reshape(CAP, rank)
+    b_down = jnp.concatenate(
+        [projected[:, 2 * block :, :rank], projected[:, 2 * block :, rank:]], axis=1
+    ).reshape(CAP, rank)
 
     def grads(left, right):
         masked = (member[:, :, None] * left[:, None, :]).reshape(CAP, nex * rank)
@@ -650,7 +667,7 @@
         and nz % 2 == 0
         and 2 < nz <= 8
         and args[0].shape[0] >= CAP
-        and CAP % (8 * nz) == 0
+        and CAP % (16 * nz) == 0
         and args[0].shape[1] % 128 == 0
         and args[2].shape[1] % 256 == 0
         and args[5].shape[1] == 64

time: 169 us -> 151 us (0.89)
  Pallas kernels: 135 us -> 121 us
  local copies, waits for them, and re-layouts: 7.05 us -> 5.12 us
  matrix products: 6.02 us -> 4.1 us
    pallas_call x1, Pallas kernels: 90.3 us -> 79.9 us  [packed_body(): pl.pallas_call(functools.partial(layer_kernel, nz, half, tiles, tile), ou...]
    pallas_call x1, Pallas kernels: 24.5 us -> 21.5 us  [packed_body(): pl.pallas_call(functools.partial(tensor_sum_kernel, nz), out_shape=jax.Sh...]
    dot_general x2, matrix products: 3.57 us -> 1.64 us  [grads(): lax.dot_general(masked, right, (((0,), (0,)), ((), ())), precision=lax.Pr...]
    concatenate x1 -> x0, local copies, waits for them, and re-layouts: 1.92 us -> none  [packed_body(): jnp.concatenate([wide[0], wide[1], wide[2], narrow, jnp.zeros((CAP, rank)...]
where the time goes in v3:
time: 151 us
  Pallas kernels  121 us (80%)
  between operations  14.9 us (10%)
  local copies, waits for them, and re-layouts  5.12 us (3%)
  other arithmetic  5.03 us (3%)
  matrix products  4.1 us (3%)
    pallas_call x1, Pallas kernels, packed_body(): pl.pallas_call(functools.partial(layer_kernel, nz, half, tiles, tile), ou...  79.9 us
    pallas_call x1, Pallas kernels, packed_body(): pl.pallas_call(functools.partial(tensor_sum_kernel, nz), out_shape=jax.Sh...  21.5 us
    pallas_call x2, Pallas kernels, small_sum(): pl.pallas_call(functools.partial(small_sum_kernel, axes, count_axes), out...  19.9 us

profile of v3, /device:TPU:0, one launch (start us, length us, event | category | flops | bytes accessed | tf_op | source)
XLA Modules:
  0.0 150.6 jit_solution(12185051560339080821)
XLA Ops:
  6.5 1.0 reduce-window.27
  7.6 0.1 slice_reduce_fusion
  7.8 0.7 broadcast_compare_fusion
  8.5 0.8 fusion.63.pick
  9.4 79.9 %layer.1.part = f32[4,200,128]{2,1,0:T(8,128)} custom-call(bf16[320,512]{1,0:T(8,128)(2,1)} %fusion.63.pick, bf16[512,1280]{1,0:T(8,128)(2,1)} %grad.1, bf16[512,1280]{1,0:T(8,128)(2,1)} %x_in.1, bf16[64,1280]{1,0:T(8,128)(2,1)} %bitcast.86, bf16[64,4352]{1,0:T(8,128)(2,1)} %bitcast.85, bf16[4352,2560]{1,0:T(8,128)(2,1)} %weight.1, bf16[512,4352]{1,0:T(8,128)(2,1)} %gate.1, ...), custom_call_target="tpu_custom_call" | custom-call | tf_op jit(solution)/shard_map/layer/pallas_call | solution.py:539
  89.3 21.5 %tensor_sum.1 = f32[4,200,128]{2,1,0:T(8,128)} custom-call(f32[4,200,128]{2,1,0:T(8,128)} %layer.1.part), custom_call_target="tpu_custom_call" | custom-call | tf_op jit(solution)/shard_map/tensor_sum/pallas_call | solution.py:570
  110.8 1.3 fusion.78
  112.3 0.2 reduce-window.29
  112.5 0.2 fusion.64
  112.7 0.1 copy.36
  112.8 0.8 fusion.56
  113.7 0.1 slice_bitcast_fusion.1
  113.8 1.1 fusion.79
  115.0 0.8 convolution_bitcast_fusion
  116.0 0.3 reshape.133
  116.3 0.6 constant_dynamic-slice_fusion.refs_0_
  116.9 0.6 reduce_sum.9
  118.2 0.6 broadcast_in_dim.8.refs_1_
  118.8 10.3 %small_sum.2 = (f32[8,3072]{1,0:T(8,128)}, f32[8,8,128]{2,1,0:T(8,128)}) custom-call(f32[8,3072]{1,0:T(8,128)} %constant_dynamic-slice_fusion.refs_0_, f32[8,128]{1,0:T(8,128)} %broadcast_in_dim.8.refs_1_), custom_call_target="tpu_custom_call" | custom-call | tf_op jit(solution)/shard_map/small_sum/pallas_call | solution.py:618
  129.1 2.2 %convolution_multiply_fusion.1.refs_0_ = f32[8,128]{1,0:T(8,128)} fusion(f32[8,3072]{1,0:T(8,128)} %get-tuple-element.52, bf16[1,128,3072]{2,1,0:T(8,128)(2,1)S(1)} %copy-done.2, f32[8]{0:T(128)S(1)} %compare_convert_fusion.1), kind=kOutput, calls=%fused_computation.69 | convolution fusion | flops 37749760 | bytes 888864 | tf_op jit(solution)/shard_map/dot_general | solution.py:635
  131.3 9.6 %small_sum.3 = f32[8,128]{1,0:T(8,128)S(1)} custom-call(f32[8,128]{1,0:T(8,128)} %convolution_multiply_fusion.1.refs_0_), custom_call_target="tpu_custom_call" | custom-call | tf_op jit(solution)/shard_map/small_sum/pallas_call | solution.py:618
  140.9 1.4 reduce_max.9
  142.9 0.2 conditional.1
  143.2 0.6 copy.45
  (21 shorter events, 0.6 us)
Async XLA Ops:
  9.4 102.9 %copy-start.8 = (s32[8]{0:T(128)S(1)}, s32[8]{0:T(128)}, u32[]{:S(2)}) copy-start(s32[8]{0:T(128)} %param.25) | copy-start | bytes 100
  89.3 27.6 %copy-start.5 = (s32[512]{0:T(512)S(1)}, s32[512]{0:T(512)}, u32[]{:S(2)}) copy-start(s32[512]{0:T(512)} %param.24) | copy-start | bytes 6148
  89.3 39.8 %copy-start.9 = (s32[8]{0:T(128)S(1)}, s32[8]{0:T(128)}, u32[]{:S(2)}) copy-start(s32[8]{0:T(128)} %param.26) | copy-start | bytes 100
  89.3 39.8 %copy-start.2 = (bf16[1,128,3072]{2,1,0:T(8,128)(2,1)S(1)}, bf16[1,128,3072]{2,1,0:T(8,128)(2,1)}, u32[]{:S(2)}) copy-start(bf16[1,128,3072]{2,1,0:T(8,128)(2,1)} %param.27) | copy-start | bytes 2359300
  89.3 53.6 %copy-start.1 = (bf16[512,1280]{1,0:T(8,128)(2,1)S(1)}, bf16[512,1280]{1,0:T(8,128)(2,1)}, u32[]{:S(2)}) copy-start(bf16[512,1280]{1,0:T(8,128)(2,1)} %grad.1) | copy-start | bytes 3932164

commit v4 on v3

--- a/solution.py
+++ b/solution.py
@@ -151,7 +151,7 @@
     width = packed.shape[1]
     rows = packed.shape[0] // PIECES
     part_rows = packed.shape[0] // 2
-    events = 2 * half
+    events = 2 * PIECES
     barrier = pltpu.get_barrier_semaphore()
     pl.semaphore_signal(barrier, inc=1, device_id={"pipe": other}, device_id_type=MESH)
     for step in (-1, 1):
@@ -236,8 +236,8 @@
         )
 
     def event(e):
-        q, i, k = e // events, (e // 2) % half, e % 2
-        j = c * i + (1 - c) * (half - 1 - i)
+        i, q, k = e // events, (e // 2) % PIECES, e % 2
+        j = jnp.where(dest == c, i * place + (1 - i) * (1 - place), c * i + (1 - c) * (1 - i))
         return j, k, q, c * half + j
 
     def receive(e):
@@ -277,12 +277,13 @@
             preferred_element_type=jnp.float32,
         )
 
-        @pl.when((t % 4 == 3) & (t // 4 < events))
-        def _():
-            receive(t // 4)
-
-    early = min(events, tiles // 4)
-    middle = events * PIECES // 2
+        @pl.when((t % 2 == 1) & (t // 2 < events))
+        def _():
+            receive(t // 2)
+
+    early = min(events, tiles // 2)
+    middle = events + PIECES
+    late = events * half - middle
 
     @pl.loop(early, middle)
     def _(e):
@@ -339,11 +340,11 @@
         def _():
             finish(s - LAG)
 
-        @pl.when((s % 2 == 1) & (s // 2 < middle))
-        def _():
-            receive(middle + s // 2)
-
-    for e in range(tiles // 2, middle):
+        @pl.when((s % 4 == 3) & (s // 4 < late))
+        def _():
+            receive(middle + s // 4)
+
+    for e in range(tiles // 4, late):
         receive(middle + e)
 
     @pl.loop(tiles, 2 * tiles)
@@ -376,7 +377,7 @@
             def _():
                 own(way, q).wait_send()
 
-    @pl.loop(0, events * PIECES)
+    @pl.loop(0, events * half)
     def _(e):
         j, k, q, source = event(e)
 
@@ -664,8 +665,7 @@
     nz = lax.axis_size("tensor")
     fits = (
         lax.axis_size("pipe") == 2
-        and nz % 2 == 0
-        and 2 < nz <= 8
+        and nz == 4
         and args[0].shape[0] >= CAP
         and CAP % (16 * nz) == 0
         and args[0].shape[1] % 128 == 0

time: 151 us -> 155 us (1.026)
  Pallas kernels: 121 us -> 125 us
    pallas_call x1, Pallas kernels: 79.9 us -> 83.4 us  [packed_body(): pl.pallas_call(functools.partial(layer_kernel, nz, half, tiles, tile), ou...]
where the time goes in v4:
time: 155 us
  Pallas kernels  125 us (81%)
  between operations  14.9 us (10%)
  local copies, waits for them, and re-layouts  5.12 us (3%)
  other arithmetic  5.03 us (3%)
  matrix products  4.1 us (3%)
    pallas_call x1, Pallas kernels, packed_body(): pl.pallas_call(functools.partial(layer_kernel, nz, half, tiles, tile), ou...  83.4 us
    pallas_call x1, Pallas kernels, packed_body(): pl.pallas_call(functools.partial(tensor_sum_kernel, nz), out_shape=jax.Sh...  21.7 us
    pallas_call x2, Pallas kernels, small_sum(): pl.pallas_call(functools.partial(small_sum_kernel, axes, count_axes), out...  20.2 us

profile of v4, /device:TPU:0, one launch (start us, length us, event | category | flops | bytes accessed | tf_op | source)
XLA Modules:
  0.0 154.7 jit_solution(9427645192035667085)
XLA Ops:
  6.5 1.0 reduce-window.27
  7.6 0.1 slice_reduce_fusion
  7.8 0.7 broadcast_compare_fusion
  8.5 0.8 fusion.63.pick
  9.4 83.4 %layer.1.part = f32[4,200,128]{2,1,0:T(8,128)} custom-call(bf16[320,512]{1,0:T(8,128)(2,1)} %fusion.63.pick, bf16[512,1280]{1,0:T(8,128)(2,1)} %grad.1, bf16[512,1280]{1,0:T(8,128)(2,1)} %x_in.1, bf16[64,1280]{1,0:T(8,128)(2,1)} %bitcast.86, bf16[64,4352]{1,0:T(8,128)(2,1)} %bitcast.85, bf16[4352,2560]{1,0:T(8,128)(2,1)} %weight.1, bf16[512,4352]{1,0:T(8,128)(2,1)} %gate.1, ...), custom_call_target="tpu_custom_call" | custom-call | tf_op jit(solution)/shard_map/layer/pallas_call | solution.py:540
  92.8 21.7 %tensor_sum.1 = f32[4,200,128]{2,1,0:T(8,128)} custom-call(f32[4,200,128]{2,1,0:T(8,128)} %layer.1.part), custom_call_target="tpu_custom_call" | custom-call | tf_op jit(solution)/shard_map/tensor_sum/pallas_call | solution.py:571
  114.6 1.3 fusion.78
  116.0 0.2 reduce-window.29
  116.2 0.2 fusion.64
  116.5 0.1 copy.36
  116.6 0.8 fusion.56
  117.4 0.1 slice_bitcast_fusion.1
  117.6 1.1 fusion.79
  118.7 0.8 convolution_bitcast_fusion
  119.7 0.3 reshape.133
  120.0 0.6 constant_dynamic-slice_fusion.refs_0_
  120.7 0.6 reduce_sum.9
  122.0 0.6 broadcast_in_dim.8.refs_1_
  122.5 10.3 %small_sum.2 = (f32[8,3072]{1,0:T(8,128)}, f32[8,8,128]{2,1,0:T(8,128)}) custom-call(f32[8,3072]{1,0:T(8,128)} %constant_dynamic-slice_fusion.refs_0_, f32[8,128]{1,0:T(8,128)} %broadcast_in_dim.8.refs_1_), custom_call_target="tpu_custom_call" | custom-call | tf_op jit(solution)/shard_map/small_sum/pallas_call | solution.py:619
  132.9 2.2 %convolution_multiply_fusion.1.refs_0_ = f32[8,128]{1,0:T(8,128)} fusion(f32[8,3072]{1,0:T(8,128)} %get-tuple-element.52, bf16[1,128,3072]{2,1,0:T(8,128)(2,1)S(1)} %copy-done.2, f32[8]{0:T(128)S(1)} %compare_convert_fusion.1), kind=kOutput, calls=%fused_computation.69 | convolution fusion | flops 37749760 | bytes 888864 | tf_op jit(solution)/shard_map/dot_general | solution.py:636
  135.1 9.9 %small_sum.3 = f32[8,128]{1,0:T(8,128)S(1)} custom-call(f32[8,128]{1,0:T(8,128)} %convolution_multiply_fusion.1.refs_0_), custom_call_target="tpu_custom_call" | custom-call | tf_op jit(solution)/shard_map/small_sum/pallas_call | solution.py:619
  145.0 1.4 reduce_max.9
  147.0 0.2 conditional.1
  147.3 0.6 copy.45
  (21 shorter events, 0.6 us)
Async XLA Ops:
  9.4 106.7 %copy-start.8 = (s32[8]{0:T(128)S(1)}, s32[8]{0:T(128)}, u32[]{:S(2)}) copy-start(s32[8]{0:T(128)} %param.25) | copy-start | bytes 100
  92.8 27.9 %copy-start.5 = (s32[512]{0:T(512)S(1)}, s32[512]{0:T(512)}, u32[]{:S(2)}) copy-start(s32[512]{0:T(512)} %param.24) | copy-start | bytes 6148
  92.8 40.0 %copy-start.9 = (s32[8]{0:T(128)S(1)}, s32[8]{0:T(128)}, u32[]{:S(2)}) copy-start(s32[8]{0:T(128)} %param.26) | copy-start | bytes 100
  92.8 40.1 %copy-start.2 = (bf16[1,128,3072]{2,1,0:T(8,128)(2,1)S(1)}, bf16[1,128,3072]{2,1,0:T(8,128)(2,1)}, u32[]{:S(2)}) copy-start(bf16[1,128,3072]{2,1,0:T(8,128)(2,1)} %param.27) | copy-start | bytes 2359300
  92.8 54.2 %copy-start.1 = (bf16[512,1280]{1,0:T(8,128)(2,1)S(1)}, bf16[512,1280]{1,0:T(8,128)(2,1)}, u32[]{:S(2)}) copy-start(bf16[512,1280]{1,0:T(8,128)(2,1)} %grad.1) | copy-start | bytes 3932164

commit v5 on v4

--- a/solution.py
+++ b/solution.py
@@ -236,7 +236,7 @@
         )
 
     def event(e):
-        i, q, k = e // events, (e // 2) % PIECES, e % 2
+        i, q, k = (e // 4) % 2, 2 * (e // 8) + (e // 2) % 2, e % 2
         j = jnp.where(dest == c, i * place + (1 - i) * (1 - place), c * i + (1 - c) * (1 - i))
         return j, k, q, c * half + j
 
@@ -282,7 +282,7 @@
             receive(t // 2)
 
     early = min(events, tiles // 2)
-    middle = events + PIECES
+    middle = events
     late = events * half - middle
 
     @pl.loop(early, middle)
@@ -340,11 +340,11 @@
         def _():
             finish(s - LAG)
 
-        @pl.when((s % 4 == 3) & (s // 4 < late))
-        def _():
-            receive(middle + s // 4)
-
-    for e in range(tiles // 4, late):
+        @pl.when((s % 2 == 1) & (s // 2 < late))
+        def _():
+            receive(middle + s // 2)
+
+    for e in range(tiles // 2, late):
         receive(middle + e)
 
     @pl.loop(tiles, 2 * tiles)

time: 155 us -> 151 us (0.974)
  Pallas kernels: 125 us -> 122 us
    pallas_call x1, Pallas kernels: 83.4 us -> 79.6 us  [packed_body(): pl.pallas_call(functools.partial(layer_kernel, nz, half, tiles, tile), ou...]
where the time goes in v5:
time: 151 us
  Pallas kernels  122 us (81%)
  between operations  14.9 us (10%)
  local copies, waits for them, and re-layouts  5.12 us (3%)
  other arithmetic  5.03 us (3%)
  matrix products  4.1 us (3%)
    pallas_call x1, Pallas kernels, packed_body(): pl.pallas_call(functools.partial(layer_kernel, nz, half, tiles, tile), ou...  79.6 us
    pallas_call x1, Pallas kernels, packed_body(): pl.pallas_call(functools.partial(tensor_sum_kernel, nz), out_shape=jax.Sh...  21.7 us
    pallas_call x2, Pallas kernels, small_sum(): pl.pallas_call(functools.partial(small_sum_kernel, axes, count_axes), out...  20.1 us

profile of v5, /device:TPU:0, one launch (start us, length us, event | category | flops | bytes accessed | tf_op | source)
XLA Modules:
  0.0 150.9 jit_solution(2856925238372176405)
XLA Ops:
  6.5 1.0 reduce-window.27
  7.6 0.1 slice_reduce_fusion
  7.8 0.7 broadcast_compare_fusion
  8.5 0.8 fusion.63.pick
  9.4 79.6 %layer.1.part = f32[4,200,128]{2,1,0:T(8,128)} custom-call(bf16[320,512]{1,0:T(8,128)(2,1)} %fusion.63.pick, bf16[512,1280]{1,0:T(8,128)(2,1)} %grad.1, bf16[512,1280]{1,0:T(8,128)(2,1)} %x_in.1, bf16[64,1280]{1,0:T(8,128)(2,1)} %bitcast.86, bf16[64,4352]{1,0:T(8,128)(2,1)} %bitcast.85, bf16[4352,2560]{1,0:T(8,128)(2,1)} %weight.1, bf16[512,4352]{1,0:T(8,128)(2,1)} %gate.1, ...), custom_call_target="tpu_custom_call" | custom-call | tf_op jit(solution)/shard_map/layer/pallas_call | solution.py:540
  89.0 21.7 %tensor_sum.1 = f32[4,200,128]{2,1,0:T(8,128)} custom-call(f32[4,200,128]{2,1,0:T(8,128)} %layer.1.part), custom_call_target="tpu_custom_call" | custom-call | tf_op jit(solution)/shard_map/tensor_sum/pallas_call | solution.py:571
  110.8 1.3 fusion.78
  112.3 0.2 reduce-window.29
  112.5 0.2 fusion.64
  112.7 0.1 copy.36
  112.8 0.8 fusion.56
  113.6 0.1 slice_bitcast_fusion.1
  113.8 1.1 fusion.79
  115.0 0.8 convolution_bitcast_fusion
  116.0 0.3 reshape.133
  116.2 0.6 constant_dynamic-slice_fusion.refs_0_
  116.9 0.6 reduce_sum.9
  118.2 0.6 broadcast_in_dim.8.refs_1_
  118.8 10.3 %small_sum.2 = (f32[8,3072]{1,0:T(8,128)}, f32[8,8,128]{2,1,0:T(8,128)}) custom-call(f32[8,3072]{1,0:T(8,128)} %constant_dynamic-slice_fusion.refs_0_, f32[8,128]{1,0:T(8,128)} %broadcast_in_dim.8.refs_1_), custom_call_target="tpu_custom_call" | custom-call | tf_op jit(solution)/shard_map/small_sum/pallas_call | solution.py:619
  129.1 2.2 %convolution_multiply_fusion.1.refs_0_ = f32[8,128]{1,0:T(8,128)} fusion(f32[8,3072]{1,0:T(8,128)} %get-tuple-element.52, bf16[1,128,3072]{2,1,0:T(8,128)(2,1)S(1)} %copy-done.2, f32[8]{0:T(128)S(1)} %compare_convert_fusion.1), kind=kOutput, calls=%fused_computation.69 | convolution fusion | flops 37749760 | bytes 888864 | tf_op jit(solution)/shard_map/dot_general | solution.py:636
  131.3 9.8 %small_sum.3 = f32[8,128]{1,0:T(8,128)S(1)} custom-call(f32[8,128]{1,0:T(8,128)} %convolution_multiply_fusion.1.refs_0_), custom_call_target="tpu_custom_call" | custom-call | tf_op jit(solution)/shard_map/small_sum/pallas_call | solution.py:619
  141.2 1.4 reduce_max.9
  143.2 0.2 conditional.1
  143.4 0.6 copy.45
  (21 shorter events, 0.6 us)
Async XLA Ops:
  9.4 102.9 %copy-start.8 = (s32[8]{0:T(128)S(1)}, s32[8]{0:T(128)}, u32[]{:S(2)}) copy-start(s32[8]{0:T(128)} %param.25) | copy-start | bytes 100
  89.0 27.9 %copy-start.5 = (s32[512]{0:T(512)S(1)}, s32[512]{0:T(512)}, u32[]{:S(2)}) copy-start(s32[512]{0:T(512)} %param.24) | copy-start | bytes 6148
  89.0 40.1 %copy-start.9 = (s32[8]{0:T(128)S(1)}, s32[8]{0:T(128)}, u32[]{:S(2)}) copy-start(s32[8]{0:T(128)} %param.26) | copy-start | bytes 100
  89.0 40.1 %copy-start.2 = (bf16[1,128,3072]{2,1,0:T(8,128)(2,1)S(1)}, bf16[1,128,3072]{2,1,0:T(8,128)(2,1)}, u32[]{:S(2)}) copy-start(bf16[1,128,3072]{2,1,0:T(8,128)(2,1)} %param.27) | copy-start | bytes 2359300
  89.0 54.1 %copy-start.1 = (bf16[512,1280]{1,0:T(8,128)(2,1)S(1)}, bf16[512,1280]{1,0:T(8,128)(2,1)}, u32[]{:S(2)}) copy-start(bf16[512,1280]{1,0:T(8,128)(2,1)} %grad.1) | copy-start | bytes 3932164
